TPU v7x, 256 devices: a whole 4x4x8 slice. The times are simulated.
256 devices in a mesh: prow: 16 (over z, core), pcol: 16 (over y, x).
Axes of the slice: x: 4, y: 4, z: 8, core: 2. Of those that a mesh axis runs over, the one named last changes fastest.
Arguments:
- factor_blocks: bfloat16 [7, 2048, 256, 256], P(None, ('prow', 'pcol')), may hold values from -0.125 to 0.125
- block_column: int32 [7, 2048], P(None, ('prow', 'pcol')), may hold values from 0 to 15
- block_row: int32 [7, 2048], P(None, ('prow', 'pcol')), may hold values from 16 to 127, as said below
- block_count: int32 [7, 256], P(None, ('prow', 'pcol')), may hold values from 1 to 8, as said below
- diag_inverse: bfloat16 [8, 256, 256, 256], P(None, ('prow', 'pcol')), as said below
- right_side: float32 [8, 256, 64, 256], P(None, ('prow', 'pcol')), may hold values from -6 to 6
Outputs:
- forward_solution: float32 [8, 256, 64, 256], P(None, ('prow', 'pcol'))
- solution: float32 [8, 256, 64, 256], P(None, ('prow', 'pcol'))
Inputs may be any that keep to these rules, and one draw needn't show every extreme that they name: Every slot of level l, live or not, names a row supernode of a later level: block_row[l, s] >= (l + 1) * 16. `block_count`: at every level some device has all 8 slots live. `diag_inverse`: each matrix is the identity plus an off-diagonal part.
All inputs are finite; a program needn't handle non-finite values.
Results may differ from a plain program's by a relative error of at most 0.015.
Values may be sent and summed in bfloat16 or wider, within the bound.
A program may use at most 128 MiB of HBM per device.

v0:
```python
import jax
import jax.numpy as jnp
from jax import lax
from jax.sharding import PartitionSpec as P


def eliminate(factor_blocks, block_column, block_row, block_count, diag_inverse, columns):
    levels = columns.shape[0]
    rhs_width = columns.shape[2]
    block_order = columns.shape[3]
    grid_cols = lax.axis_size("pcol")
    grid_rows = lax.axis_size("prow")
    slot_count = factor_blocks.shape[1]
    positions = jnp.arange(slot_count, dtype=jnp.int32)
    pending = jnp.zeros((levels * grid_cols, rhs_width, block_order), jnp.float32)
    forward = []
    for height in range(levels):
        target = columns[height, 0]
        if height > 0:
            summed = lax.psum_scatter(
                pending[height * grid_cols : (height + 1) * grid_cols],
                "pcol",
                scatter_dimension=0,
                tiled=True,
            )
            target = target - summed[0]
        solved = lax.dot_general(
            target.astype(jnp.bfloat16),
            diag_inverse[height, 0],
            (((1,), (1,)), ((), ())),
            preferred_element_type=jnp.float32,
        )
        forward.append(solved)
        if height + 1 < levels:
            blocks = lax.all_gather(solved.astype(jnp.bfloat16)[None], "prow", axis=0, tiled=True)
            picked = jnp.take(blocks, block_column[height], axis=0)
            update = jnp.einsum(
                "srb,sab->sra", picked, factor_blocks[height], preferred_element_type=jnp.float32
            )
            alive_mask = (positions < block_count[height, 0]).astype(jnp.float32)
            pending = pending.at[block_row[height]].add(update * alive_mask[:, None, None])
    rows_done = jnp.zeros((levels * grid_cols, rhs_width, block_order), jnp.bfloat16)
    result = [None] * levels
    for height in range(levels - 1, -1, -1):
        target = forward[height]
        if height + 1 < levels:
            picked = jnp.take(rows_done, block_row[height], axis=0)
            contrib = jnp.einsum(
                "sra,sab->srb", picked, factor_blocks[height], preferred_element_type=jnp.float32
            )
            alive_mask = (positions < block_count[height, 0]).astype(jnp.float32)
            gathered_terms = jnp.zeros((grid_rows, rhs_width, block_order), jnp.float32)
            gathered_terms = gathered_terms.at[block_column[height]].add(
                contrib * alive_mask[:, None, None]
            )
            summed = lax.psum_scatter(gathered_terms, "prow", scatter_dimension=0, tiled=True)
            target = target - summed[0]
        solved = jnp.dot(
            target.astype(jnp.bfloat16), diag_inverse[height, 0], preferred_element_type=jnp.float32
        )
        result[height] = solved
        if height > 0:
            arrived = lax.all_gather(solved.astype(jnp.bfloat16)[None], "pcol", axis=0, tiled=True)
            rows_done = rows_done.at[height * grid_cols : (height + 1) * grid_cols].set(arrived)
    return (jnp.stack(forward)[:, None], jnp.stack(result)[:, None])


def per_device(factor_blocks, block_column, block_row, block_count, diag_inverse, right_side):
    return eliminate(factor_blocks, block_column, block_row, block_count, diag_inverse, right_side)


def solution(mesh):
    return jax.shard_map(
        per_device,
        mesh=mesh,
        in_specs=(
            P(None, ("prow", "pcol"), None, None),
            P(None, ("prow", "pcol")),
            P(None, ("prow", "pcol")),
            P(None, ("prow", "pcol")),
            P(None, ("prow", "pcol"), None, None),
            P(None, ("prow", "pcol"), None, None),
        ),
        out_specs=(P(None, ("prow", "pcol"), None, None), P(None, ("prow", "pcol"), None, None)),
        check_vma=False,
    )
```

profile of v0, /device:TPU:1, one launch (start us, length us, event | category | flops | bytes accessed | tf_op | source)
XLA Modules:
  0.0 1351.4 jit_solution(237333425286862828)
XLA Ops:
  8.4 22.8 %all-gather = bf16[1024,256]{1,0:T(8,128)(2,1)S(1)} all-gather(bf16[64,256]{1,0:T(8,128)(2,1)S(1)} %convert_element_type.169), channel_id=2, replica_groups=mesh['prow'=16,'pcol'=16] {'prow'}, dimensions={0}, use_global_device_ids=true | all-gather | bytes 557056 | tf_op jit(solution)/shard_map/all_gather | solution.py:35
  38.3 4.3 broadcast_in_dim.52
  48.4 73.3 %reduce-scatter.43.cloned.1.call-done = f32[1,64,256]{2,1,0:T(8,128)} async-done(((f32[16,64,256]{2,1,0:T(8,128)}), f32[1,64,256]{2,1,0:T(8,128)}) %reduce-scatter.43.cloned.1.call-update) | async-done | bytes 65552
  122.8 21.0 %all-gather.1 = bf16[1024,256]{1,0:T(8,128)(2,1)S(1)} all-gather(bf16[64,256]{1,0:T(8,128)(2,1)S(1)} %convert_element_type.173), channel_id=3, replica_groups=mesh['prow'=16,'pcol'=16] {'prow'}, dimensions={0}, use_global_device_ids=true | all-gather | bytes 557056 | tf_op jit(solution)/shard_map/all_gather | solution.py:35
  151.8 72.1 %reduce-scatter.45.cloned.1.call-done = f32[1,64,256]{2,1,0:T(8,128)} async-done(((f32[16,64,256]{2,1,0:T(8,128)}), f32[1,64,256]{2,1,0:T(8,128)}) %reduce-scatter.45.cloned.1.call-update) | async-done | bytes 65552
  225.0 21.0 %all-gather.2 = bf16[1024,256]{1,0:T(8,128)(2,1)S(1)} all-gather(bf16[64,256]{1,0:T(8,128)(2,1)S(1)} %convert_element_type.177), channel_id=4, replica_groups=mesh['prow'=16,'pcol'=16] {'prow'}, dimensions={0}, use_global_device_ids=true | all-gather | bytes 557056 | tf_op jit(solution)/shard_map/all_gather | solution.py:35
  254.0 72.1 %reduce-scatter.47.cloned.1.call-done = f32[1,64,256]{2,1,0:T(8,128)} async-done(((f32[16,64,256]{2,1,0:T(8,128)}), f32[1,64,256]{2,1,0:T(8,128)}) %reduce-scatter.47.cloned.1.call-update) | async-done | bytes 65552
  327.2 21.0 %all-gather.3 = bf16[1024,256]{1,0:T(8,128)(2,1)S(1)} all-gather(bf16[64,256]{1,0:T(8,128)(2,1)S(1)} %convert_element_type.181), channel_id=5, replica_groups=mesh['prow'=16,'pcol'=16] {'prow'}, dimensions={0}, use_global_device_ids=true | all-gather | bytes 557056 | tf_op jit(solution)/shard_map/all_gather | solution.py:35
  356.2 72.1 %reduce-scatter.49.cloned.1.call-done = f32[1,64,256]{2,1,0:T(8,128)} async-done(((f32[16,64,256]{2,1,0:T(8,128)}), f32[1,64,256]{2,1,0:T(8,128)}) %reduce-scatter.49.cloned.1.call-update) | async-done | bytes 65552
  429.4 20.9 %all-gather.4 = bf16[1024,256]{1,0:T(8,128)(2,1)S(1)} all-gather(bf16[64,256]{1,0:T(8,128)(2,1)S(1)} %convert_element_type.185), channel_id=6, replica_groups=mesh['prow'=16,'pcol'=16] {'prow'}, dimensions={0}, use_global_device_ids=true | all-gather | bytes 557056 | tf_op jit(solution)/shard_map/all_gather | solution.py:35
  458.4 71.9 %reduce-scatter.51.cloned.1.call-done = f32[1,64,256]{2,1,0:T(8,128)} async-done(((f32[16,64,256]{2,1,0:T(8,128)}), f32[1,64,256]{2,1,0:T(8,128)}) %reduce-scatter.51.cloned.1.call-update) | async-done | bytes 65552
  531.4 21.0 %all-gather.5 = bf16[1024,256]{1,0:T(8,128)(2,1)S(1)} all-gather(bf16[64,256]{1,0:T(8,128)(2,1)S(1)} %convert_element_type.189), channel_id=7, replica_groups=mesh['prow'=16,'pcol'=16] {'prow'}, dimensions={0}, use_global_device_ids=true | all-gather | bytes 557056 | tf_op jit(solution)/shard_map/all_gather | solution.py:35
  560.4 72.1 %reduce-scatter.53.cloned.1.call-done = f32[1,64,256]{2,1,0:T(8,128)} async-done(((f32[16,64,256]{2,1,0:T(8,128)}), f32[1,64,256]{2,1,0:T(8,128)}) %reduce-scatter.53.cloned.1.call-update) | async-done | bytes 65552
  634.2 21.0 %all-gather.6 = bf16[1024,256]{1,0:T(8,128)(2,1)S(1)} all-gather(bf16[64,256]{1,0:T(8,128)(2,1)S(1)} %convert_element_type.193), channel_id=8, replica_groups=mesh['prow'=16,'pcol'=16] {'prow'}, dimensions={0}, use_global_device_ids=true | all-gather | bytes 557056 | tf_op jit(solution)/shard_map/all_gather | solution.py:35
  662.6 72.7 %reduce-scatter.55.cloned.1.call-done = f32[1,64,256]{2,1,0:T(8,128)} async-done(((f32[16,64,256]{2,1,0:T(8,128)}), f32[1,64,256]{2,1,0:T(8,128)}) %reduce-scatter.55.cloned.1.call-update) | async-done | bytes 65552
  737.0 17.4 %all-gather.7 = bf16[1024,256]{1,0:T(8,128)(2,1)S(1)} all-gather(bf16[64,256]{1,0:T(8,128)(2,1)S(1)} %get-tuple-element.181), channel_id=9, replica_groups=mesh['prow'=16,'pcol'=16] {'pcol'}, dimensions={0}, use_global_device_ids=true | all-gather | bytes 557056 | tf_op jit(solution)/shard_map/all_gather | solution.py:63
  756.9 2.7 gather_fusion.7
  763.5 60.7 %reduce-scatter.29.cloned.1.call-done = f32[1,64,256]{2,1,0:T(8,128)} async-done(((f32[16,64,256]{2,1,0:T(8,128)}), f32[1,64,256]{2,1,0:T(8,128)}) %reduce-scatter.29.cloned.1.call-update) | async-done | bytes 65552 | tf_op jit(solution)/shard_map/reduce_scatter | solution.py:56
  825.2 19.2 %all-gather.8 = bf16[1024,256]{1,0:T(8,128)(2,1)S(1)} all-gather(bf16[64,256]{1,0:T(8,128)(2,1)S(1)} %get-tuple-element.183), channel_id=10, replica_groups=mesh['prow'=16,'pcol'=16] {'pcol'}, dimensions={0}, use_global_device_ids=true | all-gather | bytes 557056 | tf_op jit(solution)/shard_map/all_gather | solution.py:63
  845.2 2.7 gather_fusion.8
  851.8 59.0 %reduce-scatter.31.cloned.1.call-done = f32[1,64,256]{2,1,0:T(8,128)} async-done(((f32[16,64,256]{2,1,0:T(8,128)}), f32[1,64,256]{2,1,0:T(8,128)}) %reduce-scatter.31.cloned.1.call-update) | async-done | bytes 65552 | tf_op jit(solution)/shard_map/reduce_scatter | solution.py:56
  911.7 19.3 %all-gather.9 = bf16[1024,256]{1,0:T(8,128)(2,1)S(1)} all-gather(bf16[64,256]{1,0:T(8,128)(2,1)S(1)} %get-tuple-element.185), channel_id=11, replica_groups=mesh['prow'=16,'pcol'=16] {'pcol'}, dimensions={0}, use_global_device_ids=true | all-gather | bytes 557056 | tf_op jit(solution)/shard_map/all_gather | solution.py:63
  938.4 58.8 %reduce-scatter.33.cloned.1.call-done = f32[1,64,256]{2,1,0:T(8,128)} async-done(((f32[16,64,256]{2,1,0:T(8,128)}), f32[1,64,256]{2,1,0:T(8,128)}) %reduce-scatter.33.cloned.1.call-update) | async-done | bytes 65552 | tf_op jit(solution)/shard_map/reduce_scatter | solution.py:56
  998.2 19.3 %all-gather.10 = bf16[1024,256]{1,0:T(8,128)(2,1)S(1)} all-gather(bf16[64,256]{1,0:T(8,128)(2,1)S(1)} %get-tuple-element.187), channel_id=12, replica_groups=mesh['prow'=16,'pcol'=16] {'pcol'}, dimensions={0}, use_global_device_ids=true | all-gather | bytes 557056 | tf_op jit(solution)/shard_map/all_gather | solution.py:63
  1018.3 2.7 gather_fusion.10
  1024.9 58.9 %reduce-scatter.35.cloned.1.call-done = f32[1,64,256]{2,1,0:T(8,128)} async-done(((f32[16,64,256]{2,1,0:T(8,128)}), f32[1,64,256]{2,1,0:T(8,128)}) %reduce-scatter.35.cloned.1.call-update) | async-done | bytes 65552 | tf_op jit(solution)/shard_map/reduce_scatter | solution.py:56
  1084.8 19.1 %all-gather.11 = bf16[1024,256]{1,0:T(8,128)(2,1)S(1)} all-gather(bf16[64,256]{1,0:T(8,128)(2,1)S(1)} %get-tuple-element.189), channel_id=13, replica_groups=mesh['prow'=16,'pcol'=16] {'pcol'}, dimensions={0}, use_global_device_ids=true | all-gather | bytes 557056 | tf_op jit(solution)/shard_map/all_gather | solution.py:63
  1111.3 58.8 %reduce-scatter.37.cloned.1.call-done = f32[1,64,256]{2,1,0:T(8,128)} async-done(((f32[16,64,256]{2,1,0:T(8,128)}), f32[1,64,256]{2,1,0:T(8,128)}) %reduce-scatter.37.cloned.1.call-update) | async-done | bytes 65552 | tf_op jit(solution)/shard_map/reduce_scatter | solution.py:56
  1171.1 19.3 %all-gather.12 = bf16[1024,256]{1,0:T(8,128)(2,1)S(1)} all-gather(bf16[64,256]{1,0:T(8,128)(2,1)S(1)} %get-tuple-element.191), channel_id=14, replica_groups=mesh['prow'=16,'pcol'=16] {'pcol'}, dimensions={0}, use_global_device_ids=true | all-gather | bytes 557056 | tf_op jit(solution)/shard_map/all_gather | solution.py:63
  1197.8 58.8 %reduce-scatter.39.cloned.1.call-done = f32[1,64,256]{2,1,0:T(8,128)} async-done(((f32[16,64,256]{2,1,0:T(8,128)}), f32[1,64,256]{2,1,0:T(8,128)}) %reduce-scatter.39.cloned.1.call-update) | async-done | bytes 65552 | tf_op jit(solution)/shard_map/reduce_scatter | solution.py:56
  1257.5 19.3 %all-gather.13 = bf16[1024,256]{1,0:T(8,128)(2,1)S(1)} all-gather(bf16[64,256]{1,0:T(8,128)(2,1)S(1)} %get-tuple-element.193), channel_id=15, replica_groups=mesh['prow'=16,'pcol'=16] {'pcol'}, dimensions={0}, use_global_device_ids=true | all-gather | bytes 557056 | tf_op jit(solution)/shard_map/all_gather | solution.py:63
  1284.1 58.9 %reduce-scatter.41.cloned.1.call-done = f32[1,64,256]{2,1,0:T(8,128)} async-done(((f32[16,64,256]{2,1,0:T(8,128)}), f32[1,64,256]{2,1,0:T(8,128)}) %reduce-scatter.41.cloned.1.call-update) | async-done | bytes 65552 | tf_op jit(solution)/shard_map/reduce_scatter | solution.py:56
  (188 shorter events, 122.3 us)
Async XLA Ops:
  7.2 114.6 %reduce-scatter.43.cloned.1.call-start = ((), (), s32[]{:S(2)}) async-start(), calls=%async_computation.21 | async-start | bytes 1114112
  36.5 85.2 %copy-start.7 = (bf16[8,1,256,256]{3,2,1,0:T(8,128)(2,1)S(1)}, bf16[8,1,256,256]{3,2,1,0:T(8,128)(2,1)}, u32[]{:S(2)}) copy-start(bf16[8,1,256,256]{3,2,1,0:T(8,128)(2,1)} %param.28) | copy-start | bytes 3145732
  36.5 85.2 %copy-start.8 = (f32[8,1,64,256]{3,2,1,0:T(8,128)S(1)}, f32[8,1,64,256]{3,2,1,0:T(8,128)}, u32[]{:S(2)}) copy-start(f32[8,1,64,256]{3,2,1,0:T(8,128)} %param.29) | copy-start | bytes 1572868
  47.7 176.2 %reduce-scatter.45.cloned.1.call-start = ((), (), s32[]{:S(2)}) async-start(), calls=%async_computation.22 | async-start | bytes 1114112
  151.1 175.0 %reduce-scatter.47.cloned.1.call-start = ((), (), s32[]{:S(2)}) async-start(), calls=%async_computation.23 | async-start | bytes 1114112
  253.3 175.0 %reduce-scatter.49.cloned.1.call-start = ((), (), s32[]{:S(2)}) async-start(), calls=%async_computation.24 | async-start | bytes 1114112
  355.5 174.8 %reduce-scatter.51.cloned.1.call-start = ((), (), s32[]{:S(2)}) async-start(), calls=%async_computation.25 | async-start | bytes 1114112
  356.2 174.1 %copy-start.12 = (f32[8]{0:T(128)}, f32[8]{0:T(128)S(1)}, u32[]{:S(2)}) copy-start(f32[8]{0:T(128)S(1)} %compare_convert_fusion.2) | copy-start | bytes 100
  457.7 174.8 %reduce-scatter.53.cloned.1.call-start = ((), (), s32[]{:S(2)}) async-start(), calls=%async_computation.26 | async-start | bytes 1114112
  458.4 102.0 %copy-start.14 = (f32[8]{0:T(128)}, f32[8]{0:T(128)S(1)}, u32[]{:S(2)}) copy-start(f32[8]{0:T(128)S(1)} %compare_convert_fusion.1) | copy-start | bytes 100
  531.4 101.1 %copy-start.10 = (f32[8,64,256]{2,1,0:T(8,128)}, f32[8,64,256]{2,1,0:T(8,128)S(1)}, u32[]{:S(2)}) copy-start(f32[8,64,256]{2,1,0:T(8,128)S(1)} %get-tuple-element.175) | copy-start | bytes 1572868
  552.9 109.6 %copy-start.9 = (s32[7,8]{1,0:T(8,128)S(1)}, s32[7,8]{1,0:T(8,128)}, u32[]{:S(2)}) copy-start(s32[7,8]{1,0:T(8,128)} %param.26) | copy-start | bytes 676
  559.8 175.5 %reduce-scatter.55.cloned.1.call-start = ((), (), s32[]{:S(2)}) async-start(), calls=%async_computation.27 | async-start | bytes 1114112
  657.4 104.0 %copy-start.22 = (s32[8]{0:T(128)S(1)}, s32[8]{0:T(128)}, u32[]{:S(2)}) copy-start(s32[8]{0:T(128)} %get-tuple-element.195) | copy-start | bytes 100
  662.5 185.5 %copy-start.15 = (f32[8]{0:T(128)S(1)}, f32[8]{0:T(128)}, u32[]{:S(2)}) copy-start(f32[8]{0:T(128)} %copy-done.14) | copy-start | bytes 100
  662.5 161.7 %reduce-scatter.29.cloned.1.call-start = ((), (), s32[]{:S(2)}) async-start(), calls=%async_computation.14 | async-start | bytes 1114112 | tf_op jit(solution)/shard_map/reduce_scatter | solution.py:56
  754.5 95.2 %copy-start.21 = (s32[8]{0:T(128)S(1)}, s32[8]{0:T(128)}, u32[]{:S(2)}) copy-start(s32[8]{0:T(128)} %get-tuple-element.196) | copy-start | bytes 100
  761.3 173.4 %copy-start.13 = (f32[8]{0:T(128)S(1)}, f32[8]{0:T(128)}, u32[]{:S(2)}) copy-start(f32[8]{0:T(128)} %copy-done.12) | copy-start | bytes 100
  762.4 1.0 copy-start.1
  762.4 173.9 %copy-start.20 = (s32[8]{0:T(128)S(1)}, s32[8]{0:T(128)}, u32[]{:S(2)}) copy-start(s32[8]{0:T(128)} %get-tuple-element.197) | copy-start | bytes 100
  763.4 147.3 %reduce-scatter.31.cloned.1.call-start = ((), (), s32[]{:S(2)}) async-start(), calls=%async_computation.15 | async-start | bytes 1114112 | tf_op jit(solution)/shard_map/reduce_scatter | solution.py:56
  850.7 1.0 copy-start.2
  850.7 172.0 %copy-start.19 = (s32[8]{0:T(128)S(1)}, s32[8]{0:T(128)}, u32[]{:S(2)}) copy-start(s32[8]{0:T(128)} %get-tuple-element.198) | copy-start | bytes 100
  851.7 145.5 %reduce-scatter.33.cloned.1.call-start = ((), (), s32[]{:S(2)}) async-start(), calls=%async_computation.16 | async-start | bytes 1114112 | tf_op jit(solution)/shard_map/reduce_scatter | solution.py:56
  937.4 171.8 %copy-start.18 = (s32[8]{0:T(128)S(1)}, s32[8]{0:T(128)}, u32[]{:S(2)}) copy-start(s32[8]{0:T(128)} %get-tuple-element.199) | copy-start | bytes 100
  938.4 145.5 %reduce-scatter.35.cloned.1.call-start = ((), (), s32[]{:S(2)}) async-start(), calls=%async_computation.17 | async-start | bytes 1114112 | tf_op jit(solution)/shard_map/reduce_scatter | solution.py:56
  1023.8 171.9 %copy-start.17 = (s32[8]{0:T(128)S(1)}, s32[8]{0:T(128)}, u32[]{:S(2)}) copy-start(s32[8]{0:T(128)} %get-tuple-element.201) | copy-start | bytes 100
  1024.8 145.3 %reduce-scatter.37.cloned.1.call-start = ((), (), s32[]{:S(2)}) async-start(), calls=%async_computation.18 | async-start | bytes 1114112 | tf_op jit(solution)/shard_map/reduce_scatter | solution.py:56
  1110.3 171.8 %copy-start.16 = (s32[8]{0:T(128)S(1)}, s32[8]{0:T(128)}, u32[]{:S(2)}) copy-start(s32[8]{0:T(128)} %get-tuple-element.200) | copy-start | bytes 100
  1111.2 145.3 %reduce-scatter.39.cloned.1.call-start = ((), (), s32[]{:S(2)}) async-start(), calls=%async_computation.19 | async-start | bytes 1114112 | tf_op jit(solution)/shard_map/reduce_scatter | solution.py:56
  1197.7 145.3 %reduce-scatter.41.cloned.1.call-start = ((), (), s32[]{:S(2)}) async-start(), calls=%async_computation.20 | async-start | bytes 1114112 | tf_op jit(solution)/shard_map/reduce_scatter | solution.py:56
  1283.1 1.0 copy-start
  (5 other events, 4.7 us)
Sparse Core Ops, SparseCore 0:
  47.8 73.8 reduce-scatter.42
  151.2 72.6 reduce-scatter.44
  253.4 72.6 reduce-scatter.46
  355.6 72.6 reduce-scatter.48
  457.8 72.5 reduce-scatter.50
  559.9 72.5 reduce-scatter.52
  662.6 72.5 reduce-scatter.54
  763.5 60.5 reduce-scatter.28
  851.8 58.8 reduce-scatter.30
  938.5 58.7 reduce-scatter.32
  1024.9 58.8 reduce-scatter.34
  1111.4 58.7 reduce-scatter.36
  1197.8 58.6 reduce-scatter.38
  1284.3 58.7 reduce-scatter.40
where the time goes:
time: 1360 us; the launch traced here: 1350 us
  waiting for transfers between devices  920 us (68%)
  blocking collectives  281 us (21%)
  local copies, waits for them, and re-layouts  61.5 us (5%)
  matrix products  39.2 us (3%)
  other arithmetic  33.3 us (2%)
  between operations  15 us (1%)
    unnamed x21, waiting for transfers between devices  507 us
    reduce_scatter x7, waiting for transfers between devices, eliminate(): lax.psum_scatter(gathered_terms, 'prow', scatter_dimension=0, tiled=True)  414 us
    all_gather x7, blocking collectives, eliminate(): lax.all_gather(solved.astype(jnp.bfloat16)[None], 'prow', axis=0, tiled=T...  149 us
    all_gather x7, blocking collectives, eliminate(): lax.all_gather(solved.astype(jnp.bfloat16)[None], 'pcol', axis=0, tiled=T...  133 us
  transfers between devices with their start and end apart: 14, of which 14 were waited for; matrix products, arithmetic and copies ran while one was open for 0% of the time, Pallas kernels for 0%

commit v1 on v0

v1 whole, which is shorter than its diff:
```python
import functools

import jax
import jax.numpy as jnp
from jax import lax
from jax.experimental import pallas as pl
from jax.experimental.pallas import tpu as pltpu
from jax.sharding import PartitionSpec as P

MESH = pl.DeviceIdType.MESH
CORES = 2
CHAINS = 4
TABLES = 6


def far_first(ny, nx):
    dist = lambda d, n: min(d, n - d)
    offsets = [(dy, dx) for dy in range(ny) for dx in range(nx)]
    return sorted(offsets, key=lambda o: -(dist(o[0], ny) + dist(o[1], nx)))


def ring_far_first(n):
    return sorted(range(n), key=lambda d: -min(d, n - d))


def solve_kernel(
    dims,
    factor_hbm, diag_hbm, rhs_hbm, column_ref, row_ref, count_ref,
    forward_hbm, result_hbm,
    factor, diag, rhs, y_all, x_all, rhs_first, y_first,
    gathered, picks, terms, sums, row_out, row_in, y_out,
    x_in, x_known, col_terms, col_out, col_in, x_out,
    table_own, table_land, table,
    load_sem, share_sem_s, share_sem_r, table_sem, out_sem, first_sem,
    ag_s, ag_r, rs_s, rs_r, xg_s, xg_r, cs_s, cs_r,
):
    levels, slots, nz, ny, nx, rows, order = dims
    ncol, nrow = ny * nx, CORES * nz
    half = rows // CORES
    width = half // CHAINS
    none = (levels - 1) * slots
    prow, q = lax.axis_index("prow"), lax.axis_index("pcol")
    z, core = lax.div(prow, CORES), lax.rem(prow, CORES)
    y, x = lax.div(q, nx), lax.rem(q, nx)
    other = 1 - core
    sibling = (CORES * z + other, q)
    z_far, xy_far = ring_far_first(nz), far_first(ny, nx)

    def z_partner(dz):
        return lax.rem(z + dz, nz)

    def q_partner(dy, dx):
        return lax.rem(y + dy, ny) * nx + lax.rem(x + dx, nx)

    def remote(src, dst, send, recv, device):
        pltpu.make_async_remote_copy(
            src_ref=src, dst_ref=dst, send_sem=send, recv_sem=recv, device_id=device, device_id_type=MESH
        ).start()

    def wait_for(ref, sem):
        pltpu.make_async_copy(ref, ref, sem).wait()

    def my_half(ref):
        return ref.at[:, 0, pl.ds(pl.multiple_of(core * half, half), half)]

    def other_half(ref):
        return ref.at[:, 0, pl.ds(pl.multiple_of(other * half, half), half)]

    def factor_id(level):
        return level

    def diag_id(level):
        return levels - 1 + level

    rhs_id = 2 * levels - 1

    def load_factor(level):
        i = factor_id(level)
        remote(factor_hbm.at[level], factor.at[core, level], share_sem_s.at[i], share_sem_r.at[i], sibling)
        pltpu.make_async_copy(factor_hbm.at[level], factor.at[core, level], load_sem.at[i]).start()

    def fetch_diag(level):
        pltpu.make_async_copy(diag_hbm.at[level, 0], diag.at[core, level], load_sem.at[diag_id(level)]).start()

    def share_diag(level):
        i = diag_id(level)
        remote(diag_hbm.at[level, 0], diag.at[core, level], share_sem_s.at[i], share_sem_r.at[i], sibling)

    def wait_factor(level):
        i = factor_id(level)
        wait_for(factor.at[core, level], load_sem.at[i])
        wait_for(factor.at[other, level], share_sem_r.at[i])

    def wait_diag(level):
        i = diag_id(level)
        wait_for(diag.at[core, level], load_sem.at[i])
        wait_for(diag.at[other, level], share_sem_r.at[i])

    def send_solved(level, k, found):
        y_out[k, level] = jnp.concatenate(found, axis=0).astype(jnp.bfloat16)
        for dz in z_far:
            remote(
                y_out.at[k, level], gathered.at[k, level, z],
                ag_s.at[k, level], ag_r.at[k, level], (CORES * z_partner(dz) + other, q),
            )

    barrier = pltpu.get_barrier_semaphore()
    partners = [(CORES * z_partner(dz) + other, q) for dz in z_far]
    partners += [(CORES * z + other, q_partner(*o)) for o in xy_far if o != (0, 0)]
    for device in partners:
        pl.semaphore_signal(barrier, inc=1, device_id=device, device_id_type=MESH)

    rhs_copy = pltpu.make_async_copy(rhs_hbm.at[0, 0], rhs_first, first_sem.at[0])
    rhs_copy.start()
    fetch_diag(0)
    pltpu.make_async_copy(my_half(rhs_hbm), rhs.at[core], load_sem.at[rhs_id]).start()
    zero = jnp.zeros((width, order), jnp.float32)
    for k in range(CHAINS):
        for par in range(CORES):
            sums[k, par, none] = zero
    for par in range(CORES):
        col_terms[par, slots] = zero
    rhs_copy.wait()
    wait_for(diag.at[core, 0], load_sem.at[diag_id(0)])
    solved_first = lax.dot_general(
        rhs_first[...].astype(jnp.bfloat16), diag[core, 0], (((1,), (1,)), ((), ())),
        preferred_element_type=jnp.float32,
    )
    y_first[...] = solved_first
    y_all[core, 0] = y_first[pl.ds(pl.multiple_of(core * half, half), half), :]
    index_tables(table_own, column_ref, row_ref, count_ref, levels, slots, ncol, nrow)
    pltpu.make_async_copy(table_own, table.at[core], table_sem.at[0]).start()
    pl.semaphore_wait(barrier, len(partners))

    remote(
        y_first.at[pl.ds(pl.multiple_of(other * half, half), half)], y_all.at[core, 0],
        first_sem.at[1], first_sem.at[2], sibling,
    )
    remote(table_own, table_land, table_sem.at[1], table_sem.at[2], sibling)
    wait_for(y_all.at[other, 0], first_sem.at[2])
    for k in range(CHAINS):
        found = [y_all[par, 0, pl.ds(k * width, width), :] for par in range(CORES)]
        send_solved(0, k, found)
    load_factor(0)
    remote(other_half(rhs_hbm), rhs.at[core], share_sem_s.at[rhs_id], share_sem_r.at[rhs_id], sibling)
    fetch_diag(1)
    share_diag(1)
    share_diag(0)

    def solve_forward(level, k, last):
        chain = pl.ds(k * width, width)
        wait_for(row_in.at[k, level - 1], rs_r.at[k, level - 1])
        total = row_in[k, level - 1, 0].astype(jnp.float32)
        for j in range(1, ncol):
            total += row_in[k, level - 1, j].astype(jnp.float32)
        found = []
        for par in range(CORES):
            target = rhs[par, level, chain, :] - total[par * width : (par + 1) * width]
            solved = lax.dot_general(
                target.astype(jnp.bfloat16), diag[par, level], (((1,), (1,)), ((), ())),
                preferred_element_type=jnp.float32,
            )
            y_all[par, level, chain, :] = solved
            found.append(solved)
        if not last:
            send_solved(level, k, found)

    def update_rows(level, k):
        wait_for(gathered.at[k, level], ag_r.at[k, level])
        for j in range(nz):
            arrived = gathered[k, level, j].astype(jnp.float32)
            for par in range(CORES):
                picks[CORES * j + par] = arrived[par * width : (par + 1) * width]
        for par in range(CORES):
            for s in range(slots):
                picked = picks[table[par, 0, s, level]]
                terms[par, s] = lax.dot_general(
                    picked.astype(jnp.bfloat16), factor[par, level, s], (((1,), (1,)), ((), ())),
                    preferred_element_type=jnp.float32,
                )
        for par in range(CORES):
            for s in range(slots):
                before = table[par, 2, s, level]
                sums[k, par, level * slots + s] = terms[par, s] + sums[k, par, before]
        for o in xy_far:
            r = q_partner(*o)
            both = [sums[k, par, table[par, 4, 0, (level + 1) * ncol + r]] for par in range(CORES)]
            row_out[k, level, r] = jnp.concatenate(both, axis=0).astype(jnp.bfloat16)
            remote(
                row_out.at[k, level, r], row_in.at[k, level, q],
                rs_s.at[k, level], rs_r.at[k, level], (CORES * z + other, r),
            )

    def solve_back(level, k, first, last):
        chain = pl.ds(k * width, width)
        if not first:
            wait_for(col_in.at[k, level], cs_r.at[k, level])
            total = col_in[k, level, 0].astype(jnp.float32)
            for j in range(1, nz):
                total += col_in[k, level, j].astype(jnp.float32)
        found = []
        for par in range(CORES):
            target = y_all[par, level, chain, :]
            if not first:
                target = target - total[par * width : (par + 1) * width]
            solved = jnp.dot(target.astype(jnp.bfloat16), diag[par, level], preferred_element_type=jnp.float32)
            x_all[par, level, chain, :] = solved
            found.append(solved)
        if not last:
            x_out[k, level - 1] = jnp.concatenate(found, axis=0).astype(jnp.bfloat16)
            for o in xy_far:
                r = q_partner(*o)
                remote(
                    x_out.at[k, level - 1], x_in.at[k, level - 1, q],
                    xg_s.at[k, level - 1], xg_r.at[k, level - 1], (CORES * z + other, r),
                )

    def update_columns(level, k):
        wait_for(x_in.at[k, level], xg_r.at[k, level])
        for j in range(ncol):
            arrived = x_in[k, level, j].astype(jnp.float32)
            for par in range(CORES):
                x_known[k, (level + 1) * ncol + j, par] = arrived[par * width : (par + 1) * width]
        for par in range(CORES):
            for s in range(slots):
                picked = x_known[k, table[par, 1, s, level], par]
                terms[par, s] = jnp.dot(picked.astype(jnp.bfloat16), factor[par, level, s], preferred_element_type=jnp.float32)
        for par in range(CORES):
            for s in range(slots):
                col_terms[par, s] = terms[par, s] + col_terms[par, table[par, 3, s, level]]
        for dz in z_far:
            j = z_partner(dz)
            both = []
            for par in range(CORES):
                total = col_terms[0, table[0, 5, 0, level * nrow + CORES * j + par]]
                for part in range(1, CORES):
                    total += col_terms[part, table[part, 5, 0, level * nrow + CORES * j + par]]
                both.append(total)
            col_out[k, level, j] = jnp.concatenate(both, axis=0).astype(jnp.bfloat16)
            remote(
                col_out.at[k, level, j], col_in.at[k, level, z],
                cs_s.at[k, level], cs_r.at[k, level], (CORES * j + other, q),
            )

    wait_for(table_land, table_sem.at[2])
    pltpu.make_async_copy(table_land, table.at[other], table_sem.at[3]).start()
    wait_for(table.at[core], table_sem.at[0])
    wait_for(table.at[other], table_sem.at[3])

    def forward_step(level, first, last):
        if not last:
            load_factor(level + 1)
            fetch_diag(level + 2)
            share_diag(level + 2)
        wait_factor(level)
        for k in range(CHAINS):
            update_rows(level, k)
        if first:
            wait_for(rhs.at[core], load_sem.at[rhs_id])
            wait_for(rhs.at[other], share_sem_r.at[rhs_id])
        wait_diag(level + 1)
        for k in range(CHAINS):
            solve_forward(level + 1, k, last)

    def forward_loop(level, carry):
        forward_step(level, False, False)
        return carry

    forward_step(0, True, False)
    lax.fori_loop(1, levels - 2, forward_loop, 0)
    forward_step(levels - 2, False, True)

    def give(src, out, level, sems):
        here = pl.ds(pl.multiple_of(core * half, half), half)
        pltpu.make_async_copy(src.at[core, level], out.at[level, 0, here], sems.at[0]).start()
        remote(src.at[other, level], out.at[level, 0, here], sems.at[1], sems.at[2], sibling)

    for k in range(CHAINS):
        solve_back(levels - 1, k, True, False)
    give(x_all, result_hbm, levels - 1, out_sem.at[1])
    wait_for(diag.at[other, 0], share_sem_r.at[diag_id(0)])

    def give_forward(level, carry):
        give(y_all, forward_hbm, level, out_sem.at[0])
        return carry

    lax.fori_loop(0, levels, give_forward, 0)

    def back_loop(i, carry):
        level = levels - 2 - i
        for k in range(CHAINS):
            update_columns(level, k)
        for k in range(CHAINS):
            solve_back(level, k, False, False)
        give(x_all, result_hbm, level, out_sem.at[1])
        return carry

    lax.fori_loop(0, levels - 2, back_loop, 0)
    for k in range(CHAINS):
        update_columns(0, k)
    for k in range(CHAINS):
        solve_back(0, k, False, True)
    give(x_all, result_hbm, 0, out_sem.at[1])

    def drain(level, carry):
        for k in range(CHAINS):
            wait_for(gathered.at[k, level], ag_s.at[k, level])
            wait_for(row_out.at[k, level], rs_s.at[k, level])
            wait_for(x_in.at[k, level], xg_s.at[k, level])
            wait_for(col_out.at[k, level], cs_s.at[k, level])
        wait_for(factor.at[core, level], share_sem_s.at[factor_id(level)])
        wait_for(diag.at[core, level], share_sem_s.at[diag_id(level)])
        return carry

    lax.fori_loop(0, levels - 1, drain, 0)
    wait_for(diag.at[core, levels - 1], share_sem_s.at[diag_id(levels - 1)])
    wait_for(rhs.at[core], share_sem_s.at[rhs_id])
    wait_for(table_own, table_sem.at[1])
    wait_for(y_all.at[core, 0], first_sem.at[1])
    for kind, (src, out) in enumerate(((y_all, forward_hbm), (x_all, result_hbm))):
        wait_for(src.at[core], out_sem.at[kind, 0])
        wait_for(src.at[other], out_sem.at[kind, 1])
        wait_for(other_half(out), out_sem.at[kind, 2])


def index_tables(out, column_ref, row_ref, count_ref, levels, slots, ncol, nrow):
    steps = levels - 1
    total = steps * slots
    shape = (8, 128)
    sub = lax.broadcasted_iota(jnp.int32, shape, 0)
    lane = lax.broadcasted_iota(jnp.int32, shape, 1)
    nothing = jnp.full(shape, -1, jnp.int32)
    zeros = jnp.zeros(shape, jnp.int32)
    row_of, column_of = [], []
    row_lanes, column_lanes = nothing, nothing
    rows, columns = zeros, zeros
    for level in range(steps):
        row_keys, column_keys = nothing, nothing
        row_plain, column_plain = zeros, zeros
        count = count_ref[level]
        for s in range(slots):
            row, column = row_ref[level, s], column_ref[level, s]
            live = s < count
            row_key = jnp.where(live, row, -1)
            column_key = jnp.where(live, level * nrow + column, -1)
            row_keys = jnp.where(sub == s, row_key, row_keys)
            column_keys = jnp.where(sub == s, column_key, column_keys)
            row_plain = jnp.where(sub == s, row, row_plain)
            column_plain = jnp.where(sub == s, column, column_plain)
            row_lanes = jnp.where(lane == level * slots + s, row_key, row_lanes)
            column_lanes = jnp.where(lane == level * slots + s, column_key, column_lanes)
        row_of.append(row_keys)
        column_of.append(column_keys)
        rows = jnp.where(lane == level, row_plain, rows)
        columns = jnp.where(lane == level, column_plain, columns)
    before_row, before_column = zeros, zeros
    last_row, last_column = nothing, nothing
    for level in range(steps):
        at = level * slots + sub
        earlier = lane < at
        found = jnp.max(jnp.where((row_of[level] == row_lanes) & earlier, lane, -1), axis=1, keepdims=True)
        before_row = jnp.where(lane == level, jnp.where(found < 0, total, found), before_row)
        found = jnp.max(jnp.where((column_of[level] == column_lanes) & earlier, lane, -1), axis=1, keepdims=True)
        found = jnp.where(found < level * slots, slots, found - level * slots)
        before_column = jnp.where(lane == level, found, before_column)
        valid = sub < slots
        last_row = jnp.maximum(last_row, jnp.where((row_of[level] == lane) & valid, at, -1))
        last_column = jnp.maximum(last_column, jnp.where((column_of[level] == lane) & valid, sub, -1))
    last_row = jnp.max(last_row, axis=0, keepdims=True)
    last_column = jnp.max(last_column, axis=0, keepdims=True)
    out[0] = columns
    out[1] = rows
    out[2] = before_row
    out[3] = before_column
    out[4] = jnp.broadcast_to(jnp.where(last_row < 0, total, last_row), shape)
    out[5] = jnp.broadcast_to(jnp.where(last_column < 0, slots, last_column), shape)


def deliver_kernel(forward_ref, result_ref, forward_out, result_out, stage, read_sem, write_sem):
    reads, writes = [], []
    for kind, (src, dst) in enumerate(((forward_ref, forward_out), (result_ref, result_out))):
        for level in range(src.shape[0]):
            reads.append(pltpu.make_async_copy(src.at[level], stage.at[kind, level], read_sem.at[kind, level]))
            writes.append(pltpu.make_async_copy(stage.at[kind, level], dst.at[level], write_sem.at[kind, level]))
    for read in reads:
        read.start()
    for read, write in zip(reads, writes):
        read.wait()
        write.start()
    for write in writes:
        write.wait()


def per_device(ny, nx, factor_blocks, block_column, block_row, block_count, diag_inverse, right_side):
    nrow, ncol = lax.axis_size("prow"), lax.axis_size("pcol")
    nz = nrow // CORES
    levels, _, rows, order = right_side.shape
    slots = factor_blocks.shape[1]
    half = rows // CORES
    width = half // CHAINS
    steps = levels - 1
    bf16, f32 = jnp.bfloat16, jnp.float32
    dims = (levels, slots, nz, ny, nx, rows, order)
    block, pair = (width, order), (CORES * width, order)
    dma = pltpu.SemaphoreType.DMA
    anywhere = pl.BlockSpec(memory_space=pl.ANY)
    forward, result = pl.pallas_call(
        functools.partial(solve_kernel, dims),
        name="band_solve",
        out_shape=[jax.ShapeDtypeStruct(right_side.shape, f32)] * 2,
        in_specs=[anywhere] * 3 + [pl.BlockSpec(memory_space=pltpu.SMEM)] * 3,
        out_specs=[anywhere] * 2,
        scratch_shapes=[
            pltpu.VMEM((CORES, steps, slots, order, order), bf16),
            pltpu.VMEM((CORES, levels, order, order), bf16),
            pltpu.VMEM((CORES, levels, half, order), f32),
            pltpu.VMEM((CORES, levels, half, order), f32),
            pltpu.VMEM((CORES, levels, half, order), f32),
            pltpu.VMEM((rows, order), f32),
            pltpu.VMEM((rows, order), f32),
            pltpu.VMEM((CHAINS, steps, nz) + pair, bf16),
            pltpu.VMEM((nrow,) + block, f32),
            pltpu.VMEM((CORES, slots) + block, f32),
            pltpu.VMEM((CHAINS, CORES, steps * slots + 1) + block, f32),
            pltpu.VMEM((CHAINS, steps, ncol) + pair, bf16),
            pltpu.VMEM((CHAINS, steps, ncol) + pair, bf16),
            pltpu.VMEM((CHAINS, steps) + pair, bf16),
            pltpu.VMEM((CHAINS, steps, ncol) + pair, bf16),
            pltpu.VMEM((CHAINS, levels * ncol, CORES) + block, f32),
            pltpu.VMEM((CORES, slots + 1) + block, f32),
            pltpu.VMEM((CHAINS, steps, nz) + pair, bf16),
            pltpu.VMEM((CHAINS, steps, nz) + pair, bf16),
            pltpu.VMEM((CHAINS, steps) + pair, bf16),
            pltpu.VMEM((TABLES, 8, 128), jnp.int32),
            pltpu.VMEM((TABLES, 8, 128), jnp.int32),
            pltpu.SMEM((CORES, TABLES, 8, 128), jnp.int32),
            dma((2 * levels,)),
            dma((2 * levels,)),
            dma((2 * levels,)),
            dma((4,)),
            dma((2, 3)),
            dma((3,)),
        ]
        + [dma((CHAINS, steps))] * 8,
        compiler_params=pltpu.CompilerParams(
            collective_id=0, has_side_effects=True, vmem_limit_bytes=56 * 2**20
        ),
        cost_estimate=pl.CostEstimate(
            flops=4 * rows * order * order * slots * levels, bytes_accessed=20 * 2**20, transcendentals=0
        ),
    )(factor_blocks, diag_inverse, right_side, block_column, block_row, block_count.reshape(-1))
    return pl.pallas_call(
        deliver_kernel,
        name="deliver",
        out_shape=[jax.ShapeDtypeStruct(right_side.shape, f32)] * 2,
        in_specs=[anywhere] * 2,
        out_specs=[anywhere] * 2,
        scratch_shapes=[pltpu.VMEM((2,) + right_side.shape, f32), dma((2, levels)), dma((2, levels))],
        cost_estimate=pl.CostEstimate(flops=0, bytes_accessed=2 * 2**20, transcendentals=0),
    )(forward, result)


def solution(mesh):
    ncol = mesh.shape["pcol"]
    nx = 4 if ncol % 4 == 0 else ncol
    return jax.shard_map(
        functools.partial(per_device, ncol // nx, nx),
        mesh=mesh,
        in_specs=(
            P(None, ("prow", "pcol"), None, None),
            P(None, ("prow", "pcol")),
            P(None, ("prow", "pcol")),
            P(None, ("prow", "pcol")),
            P(None, ("prow", "pcol"), None, None),
            P(None, ("prow", "pcol"), None, None),
        ),
        out_specs=(P(None, ("prow", "pcol"), None, None), P(None, ("prow", "pcol"), None, None)),
        check_vma=False,
    )
```

time: 1360 us -> 169 us (0.12)
  waiting for transfers between devices: 920 us -> 0 us
  blocking collectives: 281 us -> 0 us
  Pallas kernels: 0 us -> 167 us
  local copies, waits for them, and re-layouts: 61.5 us -> 0 us
  matrix products: 39.2 us -> 0 us
  other arithmetic: 33.3 us -> 0 us
  between operations: 15 us -> 0.8 us
    unnamed x21 -> x0, waiting for transfers between devices: 507 us -> none
    reduce_scatter x7 -> x0, waiting for transfers between devices: 414 us -> none  [eliminate(): lax.psum_scatter(gathered_terms, 'prow', scatter_dimension=0, tiled=True)]
    all_gather x14 -> x0, blocking collectives: 281 us -> none  [the longest x7 149 us: eliminate(): lax.all_gather(solved.astype(jnp.bfloat16)[None], 'prow', axis=0, tiled=T...]
    pallas_call x0 -> x2, Pallas kernels: none -> 167 us  [the longest x1 165 us: per_device(): pl.pallas_call(functools.partial(solve_kernel, dims), name='band_solve',...]
    dot_general x30 -> x0, matrix products: 39.2 us -> none  [the longest x7 11.8 us: eliminate(): jnp.einsum('srb,sab->sra', picked, factor_blocks[height], preferred_eleme...]
    scatter-add x14 -> x0, other arithmetic: 26.2 us -> none  [the longest x7 18.9 us: eliminate(): pending.at[block_row[height]].add(update * alive_mask[:, None, None])]
    gather x14 -> x0, local copies, waits for them, and re-layouts: 23.2 us -> none  [the longest x7 19.2 us: eliminate(): picked = jnp.take(rows_done, block_row[height], axis=0)]
    slice x8 -> x0, local copies, waits for them, and re-layouts: 18.3 us -> none  [the longest x7 16.7 us: eliminate(): pending[height * grid_cols:(height + 1) * grid_cols]]
  transfers between devices with their start and end apart: 14 -> 0, of which waited for: 14 -> 0; matrix products, arithmetic and copies ran while one was open for 0% -> 0% of each run, Pallas kernels for 0% -> 0%
where the time goes in v1:
time: 169 us; the launch traced here: 168 us
  Pallas kernels  167 us (99%)
    pallas_call x1, Pallas kernels, per_device(): pl.pallas_call(functools.partial(solve_kernel, dims), name='band_solve',...  165 us

profile of v1, /device:TPU:1, one launch (start us, length us, event | category | flops | bytes accessed | tf_op | source)
XLA Modules:
  0.0 168.3 jit_solution(9216438307234257370)
XLA Ops:
  0.6 165.3 %band_solve.1 = (f32[8,1,64,256]{3,2,1,0:T(8,128)}, f32[8,1,64,256]{3,2,1,0:T(8,128)}) custom-call(bf16[7,8,256,256]{3,2,1,0:T(8,128)(2,1)} %factor_hbm.1, bf16[8,1,256,256]{3,2,1,0:T(8,128)(2,1)} %diag_hbm.1, f32[8,1,64,256]{3,2,1,0:T(8,128)} %rhs_hbm.1, s32[7,8]{1,0:T(8,128)} %column_ref.1, s32[7,8]{1,0:T(8,128)} %row_ref.1, s32[7]{0:T(128)} %bitcast.1), custom_call_target="tpu_custom_call" | custom-call | flops 1073741824 | bytes 20971520 | tf_op jit(solution)/shard_map/band_solve/pallas_call | solution.py:407
  166.0 2.2 %deliver.1 = (f32[8,1,64,256]{3,2,1,0:T(8,128)}, f32[8,1,64,256]{3,2,1,0:T(8,128)}) custom-call(f32[8,1,64,256]{3,2,1,0:T(8,128)} %get-tuple-element.4.forward_ref, f32[8,1,64,256]{3,2,1,0:T(8,128)} %get-tuple-element.5.result_ref), custom_call_target="tpu_custom_call" | custom-call | bytes 2097152 | tf_op jit(solution)/shard_map/deliver/pallas_call | solution.py:452

commit v2 on v1

--- a/solution.py
+++ b/solution.py
@@ -25,13 +25,13 @@
 
 def solve_kernel(
     dims,
-    factor_hbm, diag_hbm, rhs_hbm, column_ref, row_ref, count_ref,
+    factor_hbm, diag_hbm, rhs_hbm, column_hbm, row_hbm, count_hbm,
     forward_hbm, result_hbm,
-    factor, diag, rhs, y_all, x_all, rhs_first, y_first,
+    factor, diag, rhs, y_all, x_all, rhs_first, y_first, column_ref, row_ref, count_ref,
     gathered, picks, terms, sums, row_out, row_in, y_out,
     x_in, x_known, col_terms, col_out, col_in, x_out,
     table_own, table_land, table,
-    load_sem, share_sem_s, share_sem_r, table_sem, out_sem, first_sem,
+    load_sem, share_sem_s, share_sem_r, table_sem, out_sem, first_sem, index_sem,
     ag_s, ag_r, rs_s, rs_r, xg_s, xg_r, cs_s, cs_r,
 ):
     levels, slots, nz, ny, nx, rows, order = dims
@@ -46,11 +46,8 @@
     sibling = (CORES * z + other, q)
     z_far, xy_far = ring_far_first(nz), far_first(ny, nx)
 
-    def z_partner(dz):
-        return lax.rem(z + dz, nz)
-
-    def q_partner(dy, dx):
-        return lax.rem(y + dy, ny) * nx + lax.rem(x + dx, nx)
+    z_ids = [lax.rem(z + dz, nz) for dz in z_far]
+    q_ids = [lax.rem(y + dy, ny) * nx + lax.rem(x + dx, nx) for dy, dx in xy_far]
 
     def remote(src, dst, send, recv, device):
         pltpu.make_async_remote_copy(
@@ -98,20 +95,26 @@
 
     def send_solved(level, k, found):
         y_out[k, level] = jnp.concatenate(found, axis=0).astype(jnp.bfloat16)
-        for dz in z_far:
+        for j in z_ids:
             remote(
                 y_out.at[k, level], gathered.at[k, level, z],
-                ag_s.at[k, level], ag_r.at[k, level], (CORES * z_partner(dz) + other, q),
+                ag_s.at[k, level], ag_r.at[k, level], (CORES * j + other, q),
             )
 
     barrier = pltpu.get_barrier_semaphore()
-    partners = [(CORES * z_partner(dz) + other, q) for dz in z_far]
-    partners += [(CORES * z + other, q_partner(*o)) for o in xy_far if o != (0, 0)]
+    partners = [(CORES * j + other, q) for j in z_ids]
+    partners += [(CORES * z + other, r) for r, o in zip(q_ids, xy_far) if o != (0, 0)]
     for device in partners:
         pl.semaphore_signal(barrier, inc=1, device_id=device, device_id_type=MESH)
 
     rhs_copy = pltpu.make_async_copy(rhs_hbm.at[0, 0], rhs_first, first_sem.at[0])
     rhs_copy.start()
+    index_copies = [
+        pltpu.make_async_copy(src, dst, index_sem.at[i])
+        for i, (src, dst) in enumerate(((column_hbm, column_ref), (row_hbm, row_ref), (count_hbm, count_ref)))
+    ]
+    for copy in index_copies:
+        copy.start()
     fetch_diag(0)
     pltpu.make_async_copy(my_half(rhs_hbm), rhs.at[core], load_sem.at[rhs_id]).start()
     zero = jnp.zeros((width, order), jnp.float32)
@@ -128,6 +131,8 @@
     )
     y_first[...] = solved_first
     y_all[core, 0] = y_first[pl.ds(pl.multiple_of(core * half, half), half), :]
+    for copy in index_copies:
+        copy.wait()
     index_tables(table_own, column_ref, row_ref, count_ref, levels, slots, ncol, nrow)
     pltpu.make_async_copy(table_own, table.at[core], table_sem.at[0]).start()
     pl.semaphore_wait(barrier, len(partners))
@@ -182,8 +187,7 @@
             for s in range(slots):
                 before = table[par, 2, s, level]
                 sums[k, par, level * slots + s] = terms[par, s] + sums[k, par, before]
-        for o in xy_far:
-            r = q_partner(*o)
+        for r in q_ids:
             both = [sums[k, par, table[par, 4, 0, (level + 1) * ncol + r]] for par in range(CORES)]
             row_out[k, level, r] = jnp.concatenate(both, axis=0).astype(jnp.bfloat16)
             remote(
@@ -208,8 +212,7 @@
             found.append(solved)
         if not last:
             x_out[k, level - 1] = jnp.concatenate(found, axis=0).astype(jnp.bfloat16)
-            for o in xy_far:
-                r = q_partner(*o)
+            for r in q_ids:
                 remote(
                     x_out.at[k, level - 1], x_in.at[k, level - 1, q],
                     xg_s.at[k, level - 1], xg_r.at[k, level - 1], (CORES * z + other, r),
@@ -228,8 +231,7 @@
         for par in range(CORES):
             for s in range(slots):
                 col_terms[par, s] = terms[par, s] + col_terms[par, table[par, 3, s, level]]
-        for dz in z_far:
-            j = z_partner(dz)
+        for j in z_ids:
             both = []
             for par in range(CORES):
                 total = col_terms[0, table[0, 5, 0, level * nrow + CORES * j + par]]
@@ -286,6 +288,15 @@
 
     lax.fori_loop(0, levels, give_forward, 0)
 
+    def drain(level):
+        for k in range(CHAINS):
+            wait_for(gathered.at[k, level], ag_s.at[k, level])
+            wait_for(row_out.at[k, level], rs_s.at[k, level])
+            wait_for(x_in.at[k, level], xg_s.at[k, level])
+            wait_for(col_out.at[k, level], cs_s.at[k, level])
+        wait_for(factor.at[core, level], share_sem_s.at[factor_id(level)])
+        wait_for(diag.at[core, level], share_sem_s.at[diag_id(level)])
+
     def back_loop(i, carry):
         level = levels - 2 - i
         for k in range(CHAINS):
@@ -293,30 +304,21 @@
         for k in range(CHAINS):
             solve_back(level, k, False, False)
         give(x_all, result_hbm, level, out_sem.at[1])
+        drain(level)
         return carry
 
     lax.fori_loop(0, levels - 2, back_loop, 0)
     for k in range(CHAINS):
         update_columns(0, k)
-    for k in range(CHAINS):
-        solve_back(0, k, False, True)
-    give(x_all, result_hbm, 0, out_sem.at[1])
-
-    def drain(level, carry):
-        for k in range(CHAINS):
-            wait_for(gathered.at[k, level], ag_s.at[k, level])
-            wait_for(row_out.at[k, level], rs_s.at[k, level])
-            wait_for(x_in.at[k, level], xg_s.at[k, level])
-            wait_for(col_out.at[k, level], cs_s.at[k, level])
-        wait_for(factor.at[core, level], share_sem_s.at[factor_id(level)])
-        wait_for(diag.at[core, level], share_sem_s.at[diag_id(level)])
-        return carry
-
-    lax.fori_loop(0, levels - 1, drain, 0)
+    drain(0)
     wait_for(diag.at[core, levels - 1], share_sem_s.at[diag_id(levels - 1)])
     wait_for(rhs.at[core], share_sem_s.at[rhs_id])
     wait_for(table_own, table_sem.at[1])
     wait_for(y_all.at[core, 0], first_sem.at[1])
+    for k in range(CHAINS):
+        solve_back(0, k, False, True)
+    give(x_all, result_hbm, 0, out_sem.at[1])
+
     for kind, (src, out) in enumerate(((y_all, forward_hbm), (x_all, result_hbm))):
         wait_for(src.at[core], out_sem.at[kind, 0])
         wait_for(src.at[other], out_sem.at[kind, 1])
@@ -408,7 +410,7 @@
         functools.partial(solve_kernel, dims),
         name="band_solve",
         out_shape=[jax.ShapeDtypeStruct(right_side.shape, f32)] * 2,
-        in_specs=[anywhere] * 3 + [pl.BlockSpec(memory_space=pltpu.SMEM)] * 3,
+        in_specs=[anywhere] * 3 + [anywhere] * 3,
         out_specs=[anywhere] * 2,
         scratch_shapes=[
             pltpu.VMEM((CORES, steps, slots, order, order), bf16),
@@ -418,6 +420,9 @@
             pltpu.VMEM((CORES, levels, half, order), f32),
             pltpu.VMEM((rows, order), f32),
             pltpu.VMEM((rows, order), f32),
+            pltpu.SMEM(block_column.shape, jnp.int32),
+            pltpu.SMEM(block_row.shape, jnp.int32),
+            pltpu.SMEM((steps,), jnp.int32),
             pltpu.VMEM((CHAINS, steps, nz) + pair, bf16),
             pltpu.VMEM((nrow,) + block, f32),
             pltpu.VMEM((CORES, slots) + block, f32),
@@ -440,6 +445,7 @@
             dma((4,)),
             dma((2, 3)),
             dma((3,)),
+            dma((3,)),
         ]
         + [dma((CHAINS, steps))] * 8,
         compiler_params=pltpu.CompilerParams(

time: 169 us -> 168 us (level)
  no operation moved by 1% of the time
where the time goes in v2:
time: 168 us; the launch traced here: 167 us
  Pallas kernels  166 us (99%)
    pallas_call x1, Pallas kernels, per_device(): pl.pallas_call(functools.partial(solve_kernel, dims), name='band_solve',...  164 us

profile of v2, /device:TPU:1, one launch (start us, length us, event | category | flops | bytes accessed | tf_op | source)
XLA Modules:
  0.0 167.2 jit_solution(600519156594968498)
XLA Ops:
  0.6 164.3 %band_solve.1 = (f32[8,1,64,256]{3,2,1,0:T(8,128)}, f32[8,1,64,256]{3,2,1,0:T(8,128)}) custom-call(bf16[7,8,256,256]{3,2,1,0:T(8,128)(2,1)} %factor_hbm.1, bf16[8,1,256,256]{3,2,1,0:T(8,128)(2,1)} %diag_hbm.1, f32[8,1,64,256]{3,2,1,0:T(8,128)} %rhs_hbm.1, s32[7,8]{1,0:T(8,128)} %column_hbm.1, s32[7,8]{1,0:T(8,128)} %row_hbm.1, s32[7]{0:T(128)} %bitcast.1), custom_call_target="tpu_custom_call" | custom-call | flops 1073741824 | bytes 20971520 | tf_op jit(solution)/shard_map/band_solve/pallas_call | solution.py:409
  164.9 2.2 %deliver.1 = (f32[8,1,64,256]{3,2,1,0:T(8,128)}, f32[8,1,64,256]{3,2,1,0:T(8,128)}) custom-call(f32[8,1,64,256]{3,2,1,0:T(8,128)} %get-tuple-element.4.forward_ref, f32[8,1,64,256]{3,2,1,0:T(8,128)} %get-tuple-element.5.result_ref), custom_call_target="tpu_custom_call" | custom-call | bytes 2097152 | tf_op jit(solution)/shard_map/deliver/pallas_call | solution.py:458
